TPU v7x, 512 devices: a whole 4x4x16 slice. The times are simulated.
512 devices in a mesh: inner: 16 (over z_hi, x, core), outer: 32 (over y, z_lo).
Axes of the slice: x: 4, y: 4, z: 16 (z_hi: 2, z_lo: 8; z = z_hi * 8 + z_lo), core: 2. Of those that a mesh axis runs over, the one named last changes fastest.
Arguments:
- queries: bfloat16 [65536, 1024], P(('inner', 'outer')), may hold values from -6 to 6
- keys: bfloat16 [65536, 128], P(('inner', 'outer')), may hold values from -6 to 6
- values: bfloat16 [65536, 128], P(('inner', 'outer')), may hold values from -6 to 6
- lengths: int32 [16], replicated, may hold values from 1 to 16384, 65536 in all
Outputs:
- attended: bfloat16 [65536, 1024], P(('inner', 'outer'))
Inputs may be any that keep to these rules, and one draw needn't show every extreme that they name: lengths sum to 65536; the longest is exactly 16384.
All inputs are finite; a program needn't handle non-finite values.
Results may differ from a plain program's by a relative error of at most 0.0085.
Values may be sent and summed in bfloat16 or wider, within the bound.
No kernel may reach another device: no remote copies, remote signals or barrier semaphores. Data moves between devices by JAX's collectives and lax.ppermute only.
A program may use at most 64 MiB of HBM per device.

v0:
```python
import math

import jax
import jax.numpy as jnp
from jax import lax
from jax.sharding import PartitionSpec as P


def passed_along(x, axis, by):
    size = lax.axis_size(axis)
    pairs = [(i, i + by) for i in range(size) if 0 <= i + by < size]
    return lax.ppermute(x, axis, pairs)


def doc_of(positions, ends):
    return jnp.sum((positions[:, None] >= ends[None, :]).astype(jnp.int32), axis=1)


def shards(queries, keys, values, lengths):
    tokens_here = queries.shape[0]
    head_size = keys.shape[1]
    head_count = queries.shape[1] // head_size
    outer_count = lax.axis_size("outer")
    inner_count = lax.axis_size("inner")
    row_tokens = tokens_here * outer_count
    longest = min(16384, tokens_here * outer_count * inner_count // 4)
    reach = min(inner_count - 1, (longest + row_tokens - 2) // row_tokens)
    inner_index = lax.axis_index("inner")
    outer_index = lax.axis_index("outer")
    scale = head_size ** (-0.5)
    ends = jnp.cumsum(lengths)
    query_pos = (inner_index * outer_count + outer_index) * tokens_here + jnp.arange(
        tokens_here, dtype=jnp.int32
    )
    query_doc = doc_of(query_pos, ends)
    query_mat = queries.reshape(tokens_here, head_count, head_size)

    def compute(state, key_block, value_block, first):
        peak, total, summed = state
        count = key_block.shape[0]
        key_pos = first + jnp.arange(count, dtype=jnp.int32)
        allowed = (key_pos[None, :] <= query_pos[:, None]) & (key_pos[None, :] >= 0)
        allowed = allowed & (doc_of(key_pos, ends)[None, :] == query_doc[:, None])
        scores = (
            jnp.einsum("qhd,kd->hqk", query_mat, key_block, preferred_element_type=jnp.float32)
            * scale
        )
        masked = jnp.where(allowed[None], scores, jnp.float32(-1e30))
        new_peak = jnp.maximum(peak, jnp.max(masked, axis=-1))
        weights = jnp.where(allowed[None], jnp.exp(masked - new_peak[..., None]), jnp.float32(0.0))
        factor = jnp.exp(peak - new_peak)
        total = total * factor + jnp.sum(weights, axis=-1)
        product = jnp.einsum(
            "hqk,kd->hqd",
            weights.astype(jnp.bfloat16),
            value_block,
            preferred_element_type=jnp.float32,
        )
        summed = summed * factor[..., None] + product
        return (new_peak, total, summed)

    def attend(state, key_block, value_block, first):
        return compute(state, key_block, value_block, first)

    def fold_blocks(state, key_piece, value_piece, first):
        count = key_piece.shape[0]
        size = math.gcd(count, 512)

        def visit(block_index, carry):
            key_block = lax.dynamic_slice_in_dim(key_piece, block_index * size, size, 0)
            value_block = lax.dynamic_slice_in_dim(value_piece, block_index * size, size, 0)
            return attend(carry, key_block, value_block, first + block_index * size)

        return lax.fori_loop(0, count // size, visit, state)

    state = (
        jnp.full((head_count, tokens_here), -1e30, jnp.float32),
        jnp.zeros((head_count, tokens_here), jnp.float32),
        jnp.zeros((head_count, tokens_here, head_size), jnp.float32),
    )
    stacked = jnp.stack([keys, values], axis=0)

    def fold_row(current, pair, row_start):
        piece = lax.all_gather(pair, "outer", axis=1, tiled=True)
        return fold_blocks(current, piece[0], piece[1], row_start)

    state = fold_row(state, stacked, inner_index * row_tokens)

    def turn(turn_index, carry):
        pair, current = carry
        pair = passed_along(pair, "inner", 1)
        current = fold_row(current, pair, (inner_index - turn_index) * row_tokens)
        return (pair, current)

    stacked, state = lax.fori_loop(1, reach + 1, turn, (stacked, state))
    peak, total, summed = state
    result = summed / total[..., None]
    return (
        jnp.transpose(result, (1, 0, 2))
        .reshape(tokens_here, head_count * head_size)
        .astype(jnp.bfloat16)
    )


def solution(mesh):
    in_specs = (
        P(("inner", "outer"), None),
        P(("inner", "outer"), None),
        P(("inner", "outer"), None),
        P(),
    )
    out_specs = P(("inner", "outer"), None)
    return jax.shard_map(shards, mesh=mesh, in_specs=in_specs, out_specs=out_specs, check_vma=False)
```

profile of v0, /device:TPU:36, one launch (start us, length us, event | category | flops | bytes accessed | tf_op | source)
XLA Modules:
  0.0 1308.9 jit_solution(6792853871720938636)
XLA Ops:
  6.5 1.4 pad_maximum_fusion
  8.9 1.1 copy.19
  10.3 230.6 %all-gather.3.cloned.1.call-done = bf16[2,4096,128]{2,1,0:T(8,128)(2,1)} async-done(((bf16[2,128,128]{2,1,0:T(8,128)(2,1)}), bf16[2,4096,128]{2,1,0:T(8,128)(2,1)}) %all-gather.3.cloned.1.call-update) | async-done | bytes 2097168 | tf_op jit(solution)/shard_map/all_gather | solution.py:84
  241.0 1.7 slice_bitcast_fusion.2
  242.7 18.5 %while.72 = (s32[]{:T(128)}, f32[8,128]{1,0:T(8,128)S(1)}, f32[8,128]{1,0:T(8,128)S(1)}, f32[8,128,128]{2,1,0:T(8,128)S(1)}, s32[]{:T(128)}, /*index=5*/s32[16]{...) while((s32[]{:T(128)}, f32[8,128]{1,0:T(8,128)S(1)}, ...), condition=%wide.region_6.7_spmd.clone, body=%wide.region_2.6_spmd.clone.sunk | while | flops 275937408 | bytes 8205103 | solution.py:74
  244.1 0.9 convolution_add_fusion.4
  246.4 0.9 convolution_add_fusion.4
  248.7 0.9 convolution_add_fusion.4
  253.4 0.9 convolution_add_fusion.4
  258.0 0.9 convolution_add_fusion.4
  261.2 1040.3 %while.71 = (s32[]{:T(128)}, bf16[2,128,128]{2,1,0:T(8,128)(2,1)S(1)}, f32[8,128]{1,0:T(8,128)S(1)}, f32[8,128]{1,0:T(8,128)S(1)}, f32[8,128,128]{2,1,0:T(8,128)...) while((s32[]{:T(128)}, ...), condition=%wide.region_13.14_spmd.clone, body=%wide.region_7.13_spmd.clone.sunk | while | flops 275803264 | bytes 19543228 | solution.py:95
  261.3 1.9 collective-permute-start
  263.2 3.7 collective-permute-done
  268.4 233.0 %all-gather.5.cloned.1.call-done = bf16[2,4096,128]{2,1,0:T(8,128)(2,1)} async-done(((bf16[2,128,128]{2,1,0:T(8,128)(2,1)}), bf16[2,4096,128]{2,1,0:T(8,128)(2,1)}) %all-gather.5.cloned.1.call-update) | async-done | bytes 2097168 | tf_op jit(solution)/shard_map/while/body/eval_jaxpr/all_gather | solution.py:84
  501.3 1.7 slice_bitcast_fusion.5
  503.0 18.3 %while.73 = (s32[]{:T(128)}, f32[8,128]{1,0:T(8,128)S(1)}, f32[8,128]{1,0:T(8,128)S(1)}, f32[8,128,128]{2,1,0:T(8,128)S(1)}, s32[]{:T(128)}, /*index=5*/s32[128]...) while((s32[]{:T(128)}, f32[8,128]{1,0:T(8,128)S(1)}, ...), condition=%wide.region_12.12_spmd, body=%wide.region_8.11_spmd.sunk | while | flops 275803136 | bytes 8204567 | solution.py:74
  521.3 1.9 collective-permute-start
  523.2 3.7 collective-permute-done
  528.4 233.0 %all-gather.5.cloned.1.call-done = bf16[2,4096,128]{2,1,0:T(8,128)(2,1)} async-done(((bf16[2,128,128]{2,1,0:T(8,128)(2,1)}), bf16[2,4096,128]{2,1,0:T(8,128)(2,1)}) %all-gather.5.cloned.1.call-update) | async-done | bytes 2097168 | tf_op jit(solution)/shard_map/while/body/eval_jaxpr/all_gather | solution.py:84
  761.4 1.7 slice_bitcast_fusion.5
  763.1 18.3 %while.73 = (s32[]{:T(128)}, f32[8,128]{1,0:T(8,128)S(1)}, f32[8,128]{1,0:T(8,128)S(1)}, f32[8,128,128]{2,1,0:T(8,128)S(1)}, s32[]{:T(128)}, /*index=5*/s32[128]...) while((s32[]{:T(128)}, f32[8,128]{1,0:T(8,128)S(1)}, ...), condition=%wide.region_12.12_spmd, body=%wide.region_8.11_spmd.sunk | while | flops 275803136 | bytes 8204567 | solution.py:74
  781.4 1.9 collective-permute-start
  783.3 3.7 collective-permute-done
  788.5 233.0 %all-gather.5.cloned.1.call-done = bf16[2,4096,128]{2,1,0:T(8,128)(2,1)} async-done(((bf16[2,128,128]{2,1,0:T(8,128)(2,1)}), bf16[2,4096,128]{2,1,0:T(8,128)(2,1)}) %all-gather.5.cloned.1.call-update) | async-done | bytes 2097168 | tf_op jit(solution)/shard_map/while/body/eval_jaxpr/all_gather | solution.py:84
  1021.4 1.7 slice_bitcast_fusion.5
  1023.1 18.3 %while.73 = (s32[]{:T(128)}, f32[8,128]{1,0:T(8,128)S(1)}, f32[8,128]{1,0:T(8,128)S(1)}, f32[8,128,128]{2,1,0:T(8,128)S(1)}, s32[]{:T(128)}, /*index=5*/s32[128]...) while((s32[]{:T(128)}, f32[8,128]{1,0:T(8,128)S(1)}, ...), condition=%wide.region_12.12_spmd, body=%wide.region_8.11_spmd.sunk | while | flops 275803136 | bytes 8204567 | solution.py:74
  1041.4 1.9 collective-permute-start
  1043.4 3.7 collective-permute-done
  1048.5 233.0 %all-gather.5.cloned.1.call-done = bf16[2,4096,128]{2,1,0:T(8,128)(2,1)} async-done(((bf16[2,128,128]{2,1,0:T(8,128)(2,1)}), bf16[2,4096,128]{2,1,0:T(8,128)(2,1)}) %all-gather.5.cloned.1.call-update) | async-done | bytes 2097168 | tf_op jit(solution)/shard_map/while/body/eval_jaxpr/all_gather | solution.py:84
  1281.5 1.7 slice_bitcast_fusion.5
  1283.2 18.3 %while.73 = (s32[]{:T(128)}, f32[8,128]{1,0:T(8,128)S(1)}, f32[8,128]{1,0:T(8,128)S(1)}, f32[8,128,128]{2,1,0:T(8,128)S(1)}, s32[]{:T(128)}, /*index=5*/s32[128]...) while((s32[]{:T(128)}, f32[8,128]{1,0:T(8,128)S(1)}, ...), condition=%wide.region_12.12_spmd, body=%wide.region_8.11_spmd.sunk | while | flops 275803136 | bytes 8204567 | solution.py:74
  1301.5 0.9 copy_bitcast_fusion
  (440 shorter events, 91.0 us)
Async XLA Ops:
  6.5 234.4 %all-gather.3.cloned.1.call-start = ((), (), s32[]{:S(2)}) async-start(), calls=%async_computation | async-start | bytes 2162688 | tf_op jit(solution)/shard_map/all_gather | solution.py:84
  242.6 18.5 %copy-start.1 = (bf16[2,128,128]{2,1,0:T(8,128)(2,1)S(1)}, bf16[2,128,128]{2,1,0:T(8,128)(2,1)}, u32[]{:S(2)}) copy-start(bf16[2,128,128]{2,1,0:T(8,128)(2,1)} %pad_maximum_fusion) | copy-start | bytes 196612
  261.2 240.1 %all-gather.5.cloned.1.call-start = ((), (), s32[]{:S(2)}) async-start(), calls=%async_computation.1 | async-start | bytes 2162688 | tf_op jit(solution)/shard_map/while/body/eval_jaxpr/all_gather | solution.py:84
  261.3 5.6 collective-permute-start
  266.8 0.6 copy-start
  521.3 240.1 %all-gather.5.cloned.1.call-start = ((), (), s32[]{:S(2)}) async-start(), calls=%async_computation.1 | async-start | bytes 2162688 | tf_op jit(solution)/shard_map/while/body/eval_jaxpr/all_gather | solution.py:84
  521.3 5.6 collective-permute-start
  526.9 0.6 copy-start
  781.3 240.1 %all-gather.5.cloned.1.call-start = ((), (), s32[]{:S(2)}) async-start(), calls=%async_computation.1 | async-start | bytes 2162688 | tf_op jit(solution)/shard_map/while/body/eval_jaxpr/all_gather | solution.py:84
  781.4 5.6 collective-permute-start
  787.0 0.6 copy-start
  1041.4 240.1 %all-gather.5.cloned.1.call-start = ((), (), s32[]{:S(2)}) async-start(), calls=%async_computation.1 | async-start | bytes 2162688 | tf_op jit(solution)/shard_map/while/body/eval_jaxpr/all_gather | solution.py:84
  1041.4 5.6 collective-permute-start
  1047.0 0.6 copy-start
Sparse Core Ops, SparseCore 0:
  9.4 231.4 all-gather.2
  267.6 233.6 all-gather.4
  527.7 233.6 all-gather.4
  787.7 233.6 all-gather.4
  1047.8 233.6 all-gather.4
where the time goes:
time: 1310 us
  waiting for transfers between devices  1180 us (90%)
  matrix products  51.9 us (4%)
  other arithmetic  38.6 us (3%)
  local copies, waits for them, and re-layouts  16.4 us (1%)
  between operations  13.2 us (1%)
    all_gather x5, waiting for transfers between devices, fold_row(): piece = lax.all_gather(pair, 'outer', axis=1, tiled=True)  1160 us
    dot_general x40, matrix products, compute(): jnp.einsum('hqk,kd->hqd', weights.astype(jnp.bfloat16), value_block, pref...  33.7 us
  transfers between devices with their start and end apart: 9, of which 9 were waited for; matrix products, arithmetic and copies ran while one was open for 0% of the time, Pallas kernels for 0%

commit v1 on v0

v1 whole, which is shorter than its diff:
```python
import functools
import math

import jax
import jax.numpy as jnp
from jax import lax
from jax.experimental import pallas as pl
from jax.experimental.pallas import tpu as pltpu
from jax.sharding import PartitionSpec as P

AXES = ("inner", "outer")
HEAD = 128
HEADS = 8
TOKENS = 128
ROWS = HEADS * TOKENS
SPAN = 16384
SCALE = HEAD**-0.5 * math.log2(math.e)
ROOM = 50.0
LARGEST_KEY = 6.0
HEADROOM = 100.0
LOWEST = -float(2**66)
MASKED = -1e30
STATS = 16


def coords(i):
    inner, outer = divmod(i, 32)
    return dict(zh=inner // 8, u=inner // 4 % 2, xp=inner // 2 % 2, c=inner % 2, y=outer // 8, w=outer // 2 % 4, zp=outer % 2)


def index(d):
    inner = d["zh"] * 8 + d["u"] * 4 + d["xp"] * 2 + d["c"]
    return inner * 32 + d["y"] * 8 + d["w"] * 2 + d["zp"]


def move(x, f):
    pairs = []
    for i in range(512):
        d = coords(i)
        to = f(**d)
        if to is not None:
            pairs.append((i, index({**d, **to})))
    return lax.ppermute(x, AXES, pairs)


def to_next_span(zh, u, xp, y, w, **_):
    span = 2 * zh + u + 1
    if span > 3:
        return None
    return dict(zh=span // 2, u=span % 2, xp=xp ^ (y & 1), w=3 - w if span == 2 else w)


def prep_kv_kernel(k_ref, v_ref, o_ref):
    o_ref[0] = k_ref[...]
    o_ref[1] = v_ref[...].T


def halves(x):
    high = x.astype(jnp.bfloat16).astype(jnp.float32)
    return high, (x - high).astype(jnp.bfloat16).astype(jnp.float32)


def stacked(row, *rows):
    out = jnp.zeros(row.shape, jnp.float32)
    for i, x in enumerate(rows):
        out = jnp.where(row == i, x, out)
    return out.astype(jnp.bfloat16)


def prep_q_kernel(q_ref, k_ref, o_ref):
    key_t = k_ref[...].T.astype(jnp.float32)
    row = lax.broadcasted_iota(jnp.int32, (STATS, TOKENS), 0)
    for h in range(HEADS):
        s = slice(h * HEAD, (h + 1) * HEAD)
        query_t = q_ref[:, s].T
        o_ref[:HEAD, s] = query_t
        query = query_t.astype(jnp.float32)
        shift = jnp.sum(query * key_t, axis=0, keepdims=True) * SCALE + ROOM
        high, low = halves(shift)
        highest = jnp.sum(jnp.abs(query), axis=0, keepdims=True) * (LARGEST_KEY * SCALE)
        unsafe = jnp.where(highest - shift > HEADROOM, 1.0, 0.0)
        o_ref[HEAD:, s] = stacked(row, high, low, unsafe)


def per_head(allowed, x, other):
    return jnp.concatenate(
        [jnp.where(allowed, x[:, h * TOKENS : (h + 1) * TOKENS], other) for h in range(HEADS)], axis=1
    )


def fold(pos, info, tiles, qi, q_at, qt_ref, at, row_ref, m_ref, l_ref, acc_ref):
    q_first, start_first, start_last, unsafe = (info[4 * qi + j] for j in range(4))
    for number, blocks in enumerate(tiles):

        def one(src, carry, number=number, blocks=blocks):
            places = [pos[(2 * number + src) * len(blocks) + j] for j in range(len(blocks))]
            low = functools.reduce(jnp.minimum, places)
            high = functools.reduce(jnp.maximum, places) + (TOKENS - 1)
            active = (high >= start_first) & (low <= q_first + (TOKENS - 1))
            whole = (high <= q_first) & (low >= start_last)
            safe = unsafe == 0

            def visit(masked, online):
                key = jnp.concatenate([ref[j, src, 0] for ref, j in blocks], axis=0)
                value_t = jnp.concatenate([ref[j, src, 1] for ref, j in blocks], axis=1)
                if masked:
                    iota = lax.broadcasted_iota(jnp.int32, (TOKENS, TOKENS), 0)
                    key_pos = jnp.concatenate([iota + p for p in places], axis=0)
                    allowed = (key_pos <= row_ref[q_at, 0:1]) & (key_pos >= row_ref[q_at, 1:2])
                scores = lax.dot(key, qt_ref[q_at, :HEAD], preferred_element_type=jnp.float32)
                if not online:
                    weights = jnp.exp2(scores * SCALE - m_ref[at])
                    if masked:
                        weights = per_head(allowed, weights, 0.0)
                    l_ref[at] += jnp.sum(weights, axis=0, keepdims=True)
                    acc_ref[at] += lax.dot(
                        value_t, weights.astype(jnp.bfloat16), preferred_element_type=jnp.float32
                    )
                    return
                scores = per_head(allowed, scores, MASKED)
                old = m_ref[at]
                new = jnp.maximum(old, jnp.max(scores, axis=0, keepdims=True) * SCALE)
                weights = jnp.exp2(scores * SCALE - new)
                factor = jnp.exp2(old - new)
                m_ref[at] = new
                l_ref[at] = l_ref[at] * factor + jnp.sum(weights, axis=0, keepdims=True)
                acc_ref[at] = acc_ref[at] * factor + lax.dot(
                    value_t, weights.astype(jnp.bfloat16), preferred_element_type=jnp.float32
                )

            @pl.when(active & whole & safe)
            def _():
                visit(False, False)

            @pl.when(active & jnp.logical_not(whole) & safe)
            def _():
                visit(True, False)

            @pl.when(active & jnp.logical_not(safe))
            def _():
                visit(True, True)

            return carry

        lax.fori_loop(0, 2, one, 0)


def tiles_of(shape, refs):
    return [[(refs[a], j) for a, j in blocks] for blocks in shape]


def part_kernel(shape, n, pos, info, *refs):
    tiles, (qt_ref, row_ref, m_ref, l_ref, acc_ref) = tiles_of(shape, refs), refs[n:]
    l_ref[...] = jnp.zeros_like(l_ref)
    acc_ref[...] = jnp.zeros_like(acc_ref)

    def one(qi, carry):
        rows = qt_ref[qi, HEAD:].astype(jnp.float32)
        m_ref[qi] = jnp.where(info[4 * qi + 3] == 0, rows[0:1] + rows[1:2], LOWEST)
        fold(pos, info, tiles, qi, qi, qt_ref, qi, row_ref, m_ref, l_ref, acc_ref)
        return carry

    lax.fori_loop(0, 4, one, 0)


def last_kernel(shape, n, states, qi, pos, info, *refs):
    tiles, rest = tiles_of(shape, refs), refs[n:]
    qt_ref, row_ref, *parts = rest[: 2 + 3 * states]
    out_ref, m_ref, l_ref, acc_ref = rest[2 + 3 * states :]
    peaks = [parts[3 * i][0] for i in range(states)]
    top = functools.reduce(jnp.maximum, peaks)
    factors = [jnp.exp2(p - top) for p in peaks]
    m_ref[0] = top
    l_ref[0] = sum(parts[3 * i + 1][0] * factors[i] for i in range(states))
    acc_ref[0] = sum(parts[3 * i + 2][0] * factors[i] for i in range(states))
    fold(pos, info, tiles, qi, 0, qt_ref, 0, row_ref, m_ref, l_ref, acc_ref)
    high, low = halves(m_ref[0])
    factor = jnp.exp2(m_ref[0] - (high + low))
    out_ref[:HEAD] = (acc_ref[0] * factor).astype(jnp.bfloat16)
    row = lax.broadcasted_iota(jnp.int32, (STATS, ROWS), 0)
    out_ref[HEAD:] = stacked(row, high, low, *halves(l_ref[0] * factor))


def combine_kernel(a_ref, b_ref, c_ref, d_ref, out_ref):
    refs = (a_ref, b_ref, c_ref, d_ref)
    stats = [r[HEAD:].astype(jnp.float32) for r in refs]
    peaks = [s[0:1] + s[1:2] for s in stats]
    top = functools.reduce(jnp.maximum, peaks)
    factors = [jnp.exp2(p - top) for p in peaks]
    total = sum(f * (s[2:3] + s[3:4]) for f, s in zip(factors, stats))
    inverse = [f / total for f in factors]
    for h in range(HEADS):
        s = slice(h * TOKENS, (h + 1) * TOKENS)
        summed = sum(i[:, s] * r[:HEAD, s].astype(jnp.float32) for i, r in zip(inverse, refs))
        out_ref[:, s] = summed.T.astype(jnp.bfloat16)


VMEM = pl.BlockSpec(memory_space=pltpu.VMEM)
SMEM = pl.BlockSpec(memory_space=pltpu.SMEM)


def params(mib=24):
    return pltpu.CompilerParams(vmem_limit_bytes=mib * 2**20)


def cost(tiles):
    return pl.CostEstimate(flops=tiles * 4 * 512 * ROWS * HEAD, bytes_accessed=tiles * 2**18, transcendentals=tiles * 512 * ROWS)


def state_shapes():
    return [
        jax.ShapeDtypeStruct((4, 1, ROWS), jnp.float32),
        jax.ShapeDtypeStruct((4, 1, ROWS), jnp.float32),
        jax.ShapeDtypeStruct((4, HEAD, ROWS), jnp.float32),
    ]


def part_call(shape, pos, info, arrays, qt, rows, name):
    n = len(arrays)
    return pl.pallas_call(
        functools.partial(part_kernel, shape, n),
        out_shape=state_shapes(),
        in_specs=[SMEM, SMEM] + [VMEM] * (n + 2),
        out_specs=[VMEM] * 3,
        compiler_params=params(),
        cost_estimate=cost(8),
        name=name,
    )(pos, info, *arrays, qt, rows)


def last_call(qi, shape, pos, info, arrays, qt, rows, states):
    n = len(arrays)

    def whole(dims):
        return pl.BlockSpec(dims, lambda i: (0,) * len(dims))

    def part(*dims):
        return pl.BlockSpec((1, *dims), lambda i: (qi, 0, 0))

    return pl.pallas_call(
        functools.partial(last_kernel, shape, n, len(states), qi),
        grid=(1,),
        out_shape=jax.ShapeDtypeStruct((HEAD + STATS, ROWS), jnp.bfloat16),
        in_specs=[SMEM, SMEM]
        + [whole(a.shape) for a in arrays]
        + [part(HEAD + STATS, ROWS), part(8, TOKENS)]
        + [part(1, ROWS), part(1, ROWS), part(HEAD, ROWS)] * len(states),
        out_specs=whole((HEAD + STATS, ROWS)),
        scratch_shapes=[
            pltpu.VMEM((1, 1, ROWS), jnp.float32),
            pltpu.VMEM((1, 1, ROWS), jnp.float32),
            pltpu.VMEM((1, HEAD, ROWS), jnp.float32),
        ],
        compiler_params=params(),
        cost_estimate=cost(2),
        name="last",
    )(pos, info, *arrays, qt, rows, *[x for state in states for x in state])


def shards(queries, keys, values, lengths):
    inner = lax.axis_index("inner")
    outer = lax.axis_index("outer")
    span, xp, c = inner // 4, inner // 2 % 2, inner % 2
    y, w, zp = outer // 8, outer // 2 % 4, outer % 2

    def places(cc, yy):
        out = []
        for src in range(2):
            for j in range(4):
                ww = w ^ jnp.where(cc == 0, (0, 2, 1, 3)[j], j)
                if src == 1:
                    ww = jnp.where(span == 2, 3 - ww, ww)
                out.append(
                    SPAN * (span - src) + 8192 * (xp ^ (yy & 1)) + 4096 * cc + 1024 * yy + 256 * ww + 128 * zp
                )
        return out

    def near(cc):
        return jnp.where(cc == 0, y ^ 1, 3 - y)

    def table(*lists):
        return jnp.stack([p for part in lists for p in part]).astype(jnp.int32)

    o = 1 - c
    pos_own = table(places(c, y), places(o, y))
    pos_near = table(places(c, near(c)), places(o, near(o)))
    pos_far = table(places(c, near(o)), places(c, (y + 2) % 4))
    pos_far_o = table(places(o, near(c)), places(o, (y + 2) % 4))

    ends = jnp.cumsum(lengths).astype(jnp.int32)
    q_first = jnp.stack(
        [
            SPAN * span
            + 8192 * (xp ^ jnp.where(c == 0, s // 2, s % 2))
            + 4096 * c
            + 1024 * y
            + 256 * w
            + 128 * (zp ^ jnp.where(c == 0, s % 2, s // 2))
            for s in range(4)
        ]
    ).astype(jnp.int32)
    q_pos = q_first[:, None] + jnp.arange(TOKENS, dtype=jnp.int32)[None]
    q_start = jnp.max(jnp.where(ends[None, None, :] <= q_pos[:, :, None], ends[None, None, :], 0), axis=2)
    rows = jnp.concatenate(
        [q_pos[:, None], q_start[:, None], jnp.zeros((4, 6, TOKENS), jnp.int32)], axis=1
    )

    raw = pl.pallas_call(
        prep_kv_kernel,
        out_shape=jax.ShapeDtypeStruct((2, TOKENS, HEAD), jnp.bfloat16),
        in_specs=[VMEM] * 2,
        out_specs=VMEM,
        name="prep_kv",
    )(keys, values)
    qt = pl.pallas_call(
        prep_q_kernel,
        out_shape=jax.ShapeDtypeStruct((HEAD + STATS, ROWS), jnp.bfloat16),
        in_specs=[VMEM] * 2,
        out_specs=VMEM,
        name="prep_q",
    )(queries, keys)

    with jax.named_scope("keys_x"):
        before = move(raw, to_next_span)
        mine = move(raw, lambda xp, y, **_: dict(xp=xp ^ (y & 1)))
    def to_slot(s):
        def f(c, xp, zp, **_):
            x, z = (s // 2, s % 2) if c == 0 else (s % 2, s // 2)
            return dict(xp=xp ^ x, zp=zp ^ z)

        return f

    with jax.named_scope("queries_1"):
        q1 = move(qt, to_slot(1))
    with jax.named_scope("keys_z1"):
        held = jnp.stack([mine, before])[None]
        got = move(held, lambda w, c, **_: dict(w=w ^ (1 if c else 2)))
    with jax.named_scope("queries_2"):
        q2 = jnp.stack([qt, q1])
        q4 = jnp.concatenate([q2, move(q2, to_slot(2))], axis=0)
        unsafe = jnp.max(q4[:, HEAD + 2].astype(jnp.float32), axis=1)
        unsafe = (unsafe > 0.5).astype(jnp.int32)
        info = jnp.stack([q_first, q_start[:, 0], q_start[:, -1], unsafe], axis=1).reshape(-1)
    with jax.named_scope("keys_z2"):
        held = jnp.concatenate([held, got], axis=0)
        got = move(held, lambda w, c, **_: dict(w=w ^ (2 if c else 1)))
        held = jnp.concatenate([held, got], axis=0)

    def swap(x):
        return move(x, lambda c, **_: dict(c=1 - c))

    two_arrays = tuple(tuple((a, j) for j in range(4)) for a in range(2))
    one_array = tuple(tuple((0, 4 * a + j) for j in range(4)) for a in range(2))
    with jax.named_scope("keys_y1"):
        got = move(held, lambda y, c, **_: dict(y=3 - y if c else y ^ 1))
    with jax.named_scope("keys_c0"):
        held_o = swap(held)
    with jax.named_scope("keys_y2"):
        both = jnp.concatenate([held, got], axis=0)
        far = move(both, lambda y, c, **_: dict(y=y ^ 1 if c else 3 - y))
    with jax.named_scope("keys_c1"):
        got_o = swap(got)
    states = [
        part_call(two_arrays, pos_own, info, [held, held_o], q4, rows, "own"),
        part_call(two_arrays, pos_near, info, [got, got_o], q4, rows, "near"),
    ]
    far, states = lax.optimization_barrier((far, states))
    with jax.named_scope("keys_c2"):
        far_o = swap(far)
    states.append(part_call(one_array, pos_far, info, [far], q4, rows, "far"))
    parts = []
    for s in (3, 2, 1, 0):
        part = last_call(s, one_array, pos_far_o, info, [far_o], q4, rows, states)
        if s:
            with jax.named_scope("sums"):
                part = move(part, to_slot(s))
        parts.append(part)
    return pl.pallas_call(
        combine_kernel,
        out_shape=jax.ShapeDtypeStruct((TOKENS, ROWS), jnp.bfloat16),
        in_specs=[VMEM] * 4,
        out_specs=VMEM,
        compiler_params=params(),
        name="combine",
    )(*parts)


def solution(mesh):
    spec = P(AXES, None)
    return jax.shard_map(shards, mesh=mesh, in_specs=(spec, spec, spec, P()), out_specs=spec, check_vma=False)
```

time: 1310 us -> 124 us (0.09)
  the two profiles are of different devices: /device:TPU:36 before, /device:TPU:22 now
where the time goes in v1:
time: 124 us; the launch traced here: 123 us
  starting transfers between devices  66.2 us (53%)
  Pallas kernels  33.8 us (27%)
  waiting for transfers between devices  11.8 us (10%)
  local copies, waits for them, and re-layouts  5.72 us (5%)
  other arithmetic  4.31 us (3%)
    ppermute x14, starting transfers between devices, move(): return lax.ppermute(x, AXES, pairs)  66.2 us
    pallas_call x3, Pallas kernels, part_call(): pl.pallas_call(functools.partial(part_kernel, shape, n), out_shape=state_...  19.2 us
    ppermute x14, waiting for transfers between devices, move(): return lax.ppermute(x, AXES, pairs)  11.8 us
    pallas_call x4, Pallas kernels, last_call(): pl.pallas_call(functools.partial(last_kernel, shape, n, len(states), qi),...  10.3 us
    unnamed x14, local copies, waits for them, and re-layouts  4.19 us
  transfers between devices with their start and end apart: 14, of which 3 were waited for; matrix products, arithmetic and copies ran while one was open for 5% of the time, Pallas kernels for 24%

profile of v1, /device:TPU:22, one launch (start us, length us, event | category | flops | bytes accessed | tf_op | source)
XLA Modules:
  0.0 122.6 jit_solution(88047827574260040)
XLA Ops:
  0.0 1.5 %prep_kv.1 = bf16[2,128,128]{2,1,0:T(8,128)(2,1)} custom-call(bf16[128,128]{1,0:T(8,128)(2,1)} %k_ref.3, bf16[128,128]{1,0:T(8,128)(2,1)} %v_ref.1), custom_call_target="tpu_custom_call" | custom-call | tf_op jit(solution)/shard_map/prep_kv/pallas_call | solution.py:308
  1.5 12.7 %collective-permute-start.3 = (bf16[2,128,128]{2,1,0:T(8,128)(2,1)}, bf16[2,128,128]{2,1,0:T(8,128)(2,1)S(1)}, u32[]{:S(2)}, u32[]{:S(2)}) collective-permute-start(bf16[2,128,128]{2,1,0:T(8,128)(2,1)} %prep_kv.1), channel_id=1, source_target_pairs={{0,128},{1,129},{2,130},{3,131},{4,132},{5,133},{6,134},{7,135},{8... | collective-permute-start | bytes 196616 | tf_op jit(solution)/shard_map/keys_x/ppermute | solution.py:43
  14.2 1.5 %collective-permute-start.2 = (bf16[2,128,128]{2,1,0:T(8,128)(2,1)}, bf16[2,128,128]{2,1,0:T(8,128)(2,1)S(1)}, u32[]{:S(2)}, u32[]{:S(2)}) collective-permute-start(bf16[2,128,128]{2,1,0:T(8,128)(2,1)} %prep_kv.1), channel_id=1, source_target_pairs={{0,0},{1,1},{2,2},{3,3},{4,4},{5,5},{6,6},{7,7},{8,72},{9,73},{10,... | collective-permute-start | bytes 196616 | tf_op jit(solution)/shard_map/keys_x/ppermute | solution.py:43
  15.7 1.9 %prep_q.1 = bf16[144,1024]{1,0:T(8,128)(2,1)} custom-call(bf16[128,1024]{1,0:T(8,128)(2,1)} %q_ref.1, bf16[128,128]{1,0:T(8,128)(2,1)} %k_ref.3), custom_call_target="tpu_custom_call" | custom-call | tf_op jit(solution)/shard_map/prep_q/pallas_call | solution.py:315
  17.5 3.0 %collective-permute-start = (bf16[144,1024]{1,0:T(8,128)(2,1)}, bf16[144,1024]{1,0:T(8,128)(2,1)S(1)}, u32[]{:S(2)}, u32[]{:S(2)}) collective-permute-start(bf16[144,1024]{1,0:T(8,128)(2,1)} %prep_q.1), channel_id=1, source_target_pairs={{0,1},{1,0},{2,3},{3,2},{4,5},{5,4},{6,7},{7,6},{8,9},{9,8},{10,11... | collective-permute-start | bytes 884744 | tf_op jit(solution)/shard_map/queries_1/ppermute | solution.py:43
  21.7 7.3 %collective-permute-start.4 = (bf16[1,2,2,128,128]{4,3,2,1,0:T(8,128)(2,1)S(1)}, bf16[1,2,2,128,128]{4,3,2,1,0:T(8,128)(2,1)S(1)}, u32[]{:S(2)}, u32[]{:S(2)}) collective-permute-start(bf16[1,2,2,128,128]{4,3,2,1,0:T(8,128)(2,1)S(1)} %maximum_bitcast_fusion), channel_id=1, source_target_pairs={{0,4},{1,5},{2,6},{3,7},{4,0},{5,1},{6,2},{7,3},{8,12},{9,13},{10,... | collective-permute-start | bytes 393224 | tf_op jit(solution)/shard_map/keys_z1/ppermute | solution.py:43
  29.1 4.1 %collective-permute-done.4 = bf16[1,2,2,128,128]{4,3,2,1,0:T(8,128)(2,1)S(1)} collective-permute-done((bf16[1,2,2,128,128]{4,3,2,1,0:T(8,128)(2,1)S(1)}, bf16[1,2,2,128,128]{4,3,2,1,0:T(8,128)(2,1)S(1)}, u32[]{:S(2)}, u32[]{:S(2)}) %collective-permute-start.4) | collective-permute-done | bytes 131104 | tf_op jit(solution)/shard_map/keys_z1/ppermute | solution.py:43
  33.2 5.9 %collective-permute-start.5 = (bf16[2,2,2,128,128]{4,3,2,1,0:T(8,128)(2,1)S(1)}, bf16[2,2,2,128,128]{4,3,2,1,0:T(8,128)(2,1)S(1)}, u32[]{:S(2)}, u32[]{:S(2)}) collective-permute-start(bf16[2,2,2,128,128]{4,3,2,1,0:T(8,128)(2,1)S(1)} %pad_maximum_fusion.4), channel_id=1, source_target_pairs={{0,2},{1,3},{2,0},{3,1},{4,6},{5,7},{6,4},{7,5},{8,10},{9,11},{10,... | collective-permute-start | bytes 786440 | tf_op jit(solution)/shard_map/keys_z2/ppermute | solution.py:43
  39.2 4.2 %collective-permute-done.5 = bf16[2,2,2,128,128]{4,3,2,1,0:T(8,128)(2,1)S(1)} collective-permute-done((bf16[2,2,2,128,128]{4,3,2,1,0:T(8,128)(2,1)S(1)}, bf16[2,2,2,128,128]{4,3,2,1,0:T(8,128)(2,1)S(1)}, u32[]{:S(2)}, u32[]{:S(2)}) %collective-permute-start.5) | collective-permute-done | bytes 262176 | tf_op jit(solution)/shard_map/keys_z2/ppermute | solution.py:43
  43.5 4.0 %collective-permute-start.6 = (bf16[4,2,2,128,128]{4,3,2,1,0:T(8,128)(2,1)S(1)}, bf16[4,2,2,128,128]{4,3,2,1,0:T(8,128)(2,1)}, u32[]{:S(2)}, u32[]{:S(2)}) collective-permute-start(bf16[4,2,2,128,128]{4,3,2,1,0:T(8,128)(2,1)S(1)} %pad_maximum_fusion.3.refs_0_), channel_id=1, source_target_pairs={{0,8},{1,9},{2,10},{3,11},{4,12},{5,13},{6,14},{7,15},{8,0},{9,1},... | collective-permute-start | bytes 1572872 | tf_op jit(solution)/shard_map/keys_y1/ppermute | solution.py:43
  47.6 8.4 %collective-permute-start.1 = (bf16[2,144,1024]{2,1,0:T(8,128)(2,1)S(1)}, bf16[2,144,1024]{2,1,0:T(8,128)(2,1)}, u32[]{:S(2)}, u32[]{:S(2)}) collective-permute-start(bf16[2,144,1024]{2,1,0:T(8,128)(2,1)S(1)} %pad_maximum_fusion.2), channel_id=1, source_target_pairs={{0,64},{1,65},{2,66},{3,67},{4,68},{5,69},{6,70},{7,71},{8,72},{9,... | collective-permute-start | bytes 1769480 | tf_op jit(solution)/shard_map/queries_2/ppermute | solution.py:43
  56.2 2.1 %pad_maximum_fusion.1 = bf16[8,2,2,128,128]{4,3,2,1,0:T(8,128)(2,1)} fusion(bf16[4,2,2,128,128]{4,3,2,1,0:T(8,128)(2,1)} %collective-permute-done.6.refs_0_, bf16[2,2,2,128,128]{4,3,2,1,0:T(8,128)(2,1)S(1)} %collective-permute-done.5, bf16[1,2,2,128,128]{4,3,2,1,0:T(8,128)(2,1)S(1)} %collective-permute-done.4, ...), kind=kLoop, calls=%fused_computation.1 | loop fusion | flops 1572864 | bytes 2097152 | tf_op jit(solution)/shard_map/keys_y2/concatenate | solution.py:359
  58.4 2.8 %collective-permute-start.7 = (bf16[8,2,2,128,128]{4,3,2,1,0:T(8,128)(2,1)}, bf16[8,2,2,128,128]{4,3,2,1,0:T(8,128)(2,1)}, u32[]{:S(2)}, u32[]{:S(2)}) collective-permute-start(bf16[8,2,2,128,128]{4,3,2,1,0:T(8,128)(2,1)} %pad_maximum_fusion.1), channel_id=1, source_target_pairs={{0,24},{1,25},{2,26},{3,27},{4,28},{5,29},{6,30},{7,31},{8,16},{9,... | collective-permute-start | bytes 3145736 | tf_op jit(solution)/shard_map/keys_y2/ppermute | solution.py:43
  61.7 6.0 %collective-permute-start.8 = (bf16[4,2,2,128,128]{4,3,2,1,0:T(8,128)(2,1)S(1)}, bf16[4,2,2,128,128]{4,3,2,1,0:T(8,128)(2,1)S(1)}, u32[]{:S(2)}, u32[]{:S(2)}) collective-permute-start(bf16[4,2,2,128,128]{4,3,2,1,0:T(8,128)(2,1)S(1)} %pad_maximum_fusion.3.refs_0_), channel_id=1, source_target_pairs={{0,32},{1,33},{2,34},{3,35},{4,36},{5,37},{6,38},{7,39},{8,40},{9,... | collective-permute-start | bytes 1572872 | tf_op jit(solution)/shard_map/keys_c0/ppermute | solution.py:43
  67.7 1.2 pad_maximum_fusion.refs_2_.refs_1_
  69.0 1.9 %collective-permute-start.9 = (bf16[4,2,2,128,128]{4,3,2,1,0:T(8,128)(2,1)}, bf16[4,2,2,128,128]{4,3,2,1,0:T(8,128)(2,1)}, u32[]{:S(2)}, u32[]{:S(2)}) collective-permute-start(bf16[4,2,2,128,128]{4,3,2,1,0:T(8,128)(2,1)} %collective-permute-done.6.refs_0_), channel_id=1, source_target_pairs={{0,32},{1,33},{2,34},{3,35},{4,36},{5,37},{6,38},{7,39},{8,40},{9,... | collective-permute-start | bytes 1572872 | tf_op jit(solution)/shard_map/keys_c1/ppermute | solution.py:43
  72.0 1.0 copy-done.3
  73.0 1.0 copy-done.5
  74.1 8.7 %own.1 = (f32[4,1,1024]{2,1,0:T(1,128)S(1)}, f32[4,1,1024]{2,1,0:T(1,128)S(1)}, f32[4,128,1024]{2,1,0:T(8,128)S(1)}) custom-call(s32[16]{0:T(128)S(1)} %stack.290.pos, s32[16]{0:T(128)S(1)} %reshape.93.info, bf16[4,2,2,128,128]{4,3,2,1,0:T(8,128)(2,1)S(1)} %copy-done.3, bf16[4,2,2,128,128]{4,3,2,1,0:T(8,128)(2,1)S(1)} %copy-done.5, ...), custom_call_target="tpu_custom_call" | custom-call | flops 2147483648 | bytes 2097152 | tf_op jit(solution)/shard_map/own/pallas_call | solution.py:220
  82.8 4.5 %near.1 = (f32[4,1,1024]{2,1,0:T(1,128)S(1)}, f32[4,1,1024]{2,1,0:T(1,128)S(1)}, f32[4,128,1024]{2,1,0:T(8,128)S(1)}) custom-call(s32[16]{0:T(128)S(1)} %stack.307.pos, s32[16]{0:T(128)S(1)} %reshape.93.info, bf16[4,2,2,128,128]{4,3,2,1,0:T(8,128)(2,1)} %collective-permute-done.6.refs_0_, bf16[4,2,2,128,128]{4,3,2,1,0:T(8,128)(2,1)} %collective-permute-done.9.refs_1_, ...), custom_call_target="tpu_custom_call" | custom-call | flops 2147483648 | bytes 2097152 | tf_op jit(solution)/shard_map/near/pallas_call | solution.py:220
  87.3 1.3 %copy-done = f32[4,128,1024]{2,1,0:T(8,128)} copy-done((f32[4,128,1024]{2,1,0:T(8,128)}, f32[4,128,1024]{2,1,0:T(8,128)S(1)}, u32[]{:S(2)}) %copy-start) | copy-done | bytes 2097176
  88.6 2.1 %collective-permute-start.10 = (bf16[8,2,2,128,128]{4,3,2,1,0:T(8,128)(2,1)}, bf16[8,2,2,128,128]{4,3,2,1,0:T(8,128)(2,1)}, u32[]{:S(2)}, u32[]{:S(2)}) collective-permute-start(bf16[8,2,2,128,128]{4,3,2,1,0:T(8,128)(2,1)} %collective-permute-done.7.refs_0_), channel_id=1, source_target_pairs={{0,32},{1,33},{2,34},{3,35},{4,36},{5,37},{6,38},{7,39},{8,40},{9,... | collective-permute-start | bytes 3145736 | tf_op jit(solution)/shard_map/keys_c2/ppermute | solution.py:43
  91.0 6.0 %far.1 = (f32[4,1,1024]{2,1,0:T(1,128)S(1)}, f32[4,1,1024]{2,1,0:T(1,128)S(1)}, f32[4,128,1024]{2,1,0:T(8,128)S(1)}) custom-call(s32[16]{0:T(128)S(1)} %stack.324.pos, s32[16]{0:T(128)S(1)} %reshape.93.info, bf16[8,2,2,128,128]{4,3,2,1,0:T(8,128)(2,1)} %collective-permute-done.7.refs_0_, bf16[4,144,1024]{2,1,0:T(8,128)(2,1)S(1)} %pad_maximum_fusion.refs_2_.refs_1_, ...), custom_call_target="tpu_custom_call" | custom-call | flops 2147483648 | bytes 2097152 | tf_op jit(solution)/shard_map/far/pallas_call | solution.py:220
  97.0 2.2 %last.4 = bf16[144,1024]{1,0:T(8,128)(2,1)S(1)} custom-call(s32[16]{0:T(128)S(1)} %stack.260.pos, s32[16]{0:T(128)S(1)} %reshape.93.info, bf16[8,2,2,128,128]{4,3,2,1,0:T(8,128)(2,1)} %collective-permute-done.10.refs_0_, bf16[4,144,1024]{2,1,0:T(8,128)(2,1)S(1)} %pad_maximum_fusion.refs_2_.refs_1_, s32[4,8,128]{2,1,0:T(8,128)S(1)} %add_add_fusion.refs_3_.refs_2_, ...), custom_call_target="tpu_custom_call" | custom-call | flops 536870912 | bytes 524288 | tf_op jit(solution)/shard_map/last/pallas_call | solution.py:240
  99.3 5.1 %collective-permute-start.11 = (bf16[144,1024]{1,0:T(8,128)(2,1)S(1)}, bf16[144,1024]{1,0:T(8,128)(2,1)S(1)}, u32[]{:S(2)}, u32[]{:S(2)}) collective-permute-start(bf16[144,1024]{1,0:T(8,128)(2,1)S(1)} %last.4), channel_id=1, source_target_pairs={{0,65},{1,64},{2,67},{3,66},{4,69},{5,68},{6,71},{7,70},{8,73},{9,... | collective-permute-start | bytes 884744 | tf_op jit(solution)/shard_map/sums/ppermute | solution.py:43
  104.4 2.2 %last.5 = bf16[144,1024]{1,0:T(8,128)(2,1)S(1)} custom-call(s32[16]{0:T(128)S(1)} %stack.260.pos, s32[16]{0:T(128)S(1)} %reshape.93.info, bf16[8,2,2,128,128]{4,3,2,1,0:T(8,128)(2,1)} %collective-permute-done.10.refs_0_, bf16[4,144,1024]{2,1,0:T(8,128)(2,1)S(1)} %pad_maximum_fusion.refs_2_.refs_1_, s32[4,8,128]{2,1,0:T(8,128)S(1)} %add_add_fusion.refs_3_.refs_2_, ...), custom_call_target="tpu_custom_call" | custom-call | flops 536870912 | bytes 524288 | tf_op jit(solution)/shard_map/last/pallas_call | solution.py:240
  106.6 3.4 %collective-permute-start.12 = (bf16[144,1024]{1,0:T(8,128)(2,1)S(1)}, bf16[144,1024]{1,0:T(8,128)(2,1)S(1)}, u32[]{:S(2)}, u32[]{:S(2)}) collective-permute-start(bf16[144,1024]{1,0:T(8,128)(2,1)S(1)} %last.5), channel_id=1, source_target_pairs={{0,64},{1,65},{2,66},{3,67},{4,68},{5,69},{6,70},{7,71},{8,72},{9,... | collective-permute-start | bytes 884744 | tf_op jit(solution)/shard_map/sums/ppermute | solution.py:43
  110.0 2.9 %last.6 = bf16[144,1024]{1,0:T(8,128)(2,1)S(1)} custom-call(s32[16]{0:T(128)S(1)} %stack.260.pos, s32[16]{0:T(128)S(1)} %reshape.93.info, bf16[8,2,2,128,128]{4,3,2,1,0:T(8,128)(2,1)} %collective-permute-done.10.refs_0_, bf16[4,144,1024]{2,1,0:T(8,128)(2,1)S(1)} %pad_maximum_fusion.refs_2_.refs_1_, s32[4,8,128]{2,1,0:T(8,128)S(1)} %add_add_fusion.refs_3_.refs_2_, ...), custom_call_target="tpu_custom_call" | custom-call | flops 536870912 | bytes 524288 | tf_op jit(solution)/shard_map/last/pallas_call | solution.py:240
  112.9 2.2 %collective-permute-start.13 = (bf16[144,1024]{1,0:T(8,128)(2,1)S(1)}, bf16[144,1024]{1,0:T(8,128)(2,1)S(1)}, u32[]{:S(2)}, u32[]{:S(2)}) collective-permute-start(bf16[144,1024]{1,0:T(8,128)(2,1)S(1)} %last.6), channel_id=1, source_target_pairs={{0,1},{1,0},{2,3},{3,2},{4,5},{5,4},{6,7},{7,6},{8,9},{9,8},{10,11... | collective-permute-start | bytes 884744 | tf_op jit(solution)/shard_map/sums/ppermute | solution.py:43
  115.1 2.9 %last.7.d_ref = bf16[144,1024]{1,0:T(8,128)(2,1)S(1)} custom-call(s32[16]{0:T(128)S(1)} %stack.260.pos, s32[16]{0:T(128)S(1)} %reshape.93.info, bf16[8,2,2,128,128]{4,3,2,1,0:T(8,128)(2,1)} %collective-permute-done.10.refs_0_, bf16[4,144,1024]{2,1,0:T(8,128)(2,1)S(1)} %pad_maximum_fusion.refs_2_.refs_1_, s32[4,8,128]{2,1,0:T(8,128)S(1)} %add_add_fusion.refs_3_.refs_2_, ...), custom_call_target="tpu_custom_call" | custom-call | flops 536870912 | bytes 524288 | tf_op jit(solution)/shard_map/last/pallas_call | solution.py:240
  118.1 3.5 %collective-permute-done.13.c_ref = bf16[144,1024]{1,0:T(8,128)(2,1)S(1)} collective-permute-done((bf16[144,1024]{1,0:T(8,128)(2,1)S(1)}, bf16[144,1024]{1,0:T(8,128)(2,1)S(1)}, u32[]{:S(2)}, u32[]{:S(2)}) %collective-permute-start.13) | collective-permute-done | bytes 294944 | tf_op jit(solution)/shard_map/sums/ppermute | solution.py:43
  121.6 1.0 combine.1
  (48 shorter events, 3.3 us)
Async XLA Ops:
  1.5 20.2 %collective-permute-start.3 = (bf16[2,128,128]{2,1,0:T(8,128)(2,1)}, bf16[2,128,128]{2,1,0:T(8,128)(2,1)S(1)}, u32[]{:S(2)}, u32[]{:S(2)}) collective-permute-start(bf16[2,128,128]{2,1,0:T(8,128)(2,1)} %prep_kv.1), channel_id=1, source_target_pairs={{0,128},{1,129},{2,130},{3,131},{4,132},{5,133},{6,134},{7,135},{8... | collective-permute-start | bytes 196616 | tf_op jit(solution)/shard_map/keys_x/ppermute | solution.py:43
  14.2 7.5 %collective-permute-start.2 = (bf16[2,128,128]{2,1,0:T(8,128)(2,1)}, bf16[2,128,128]{2,1,0:T(8,128)(2,1)S(1)}, u32[]{:S(2)}, u32[]{:S(2)}) collective-permute-start(bf16[2,128,128]{2,1,0:T(8,128)(2,1)} %prep_kv.1), channel_id=1, source_target_pairs={{0,0},{1,1},{2,2},{3,3},{4,4},{5,5},{6,6},{7,7},{8,72},{9,73},{10,... | collective-permute-start | bytes 196616 | tf_op jit(solution)/shard_map/keys_x/ppermute | solution.py:43
  17.5 30.0 %copy-start.6 = (bf16[144,1024]{1,0:T(8,128)(2,1)S(1)}, bf16[144,1024]{1,0:T(8,128)(2,1)}, u32[]{:S(2)}) copy-start(bf16[144,1024]{1,0:T(8,128)(2,1)} %prep_q.1) | copy-start | bytes 884740
  17.5 30.0 %collective-permute-start = (bf16[144,1024]{1,0:T(8,128)(2,1)}, bf16[144,1024]{1,0:T(8,128)(2,1)S(1)}, u32[]{:S(2)}, u32[]{:S(2)}) collective-permute-start(bf16[144,1024]{1,0:T(8,128)(2,1)} %prep_q.1), channel_id=1, source_target_pairs={{0,1},{1,0},{2,3},{3,2},{4,5},{5,4},{6,7},{7,6},{8,9},{9,8},{10,11... | collective-permute-start | bytes 884744 | tf_op jit(solution)/shard_map/queries_1/ppermute | solution.py:43
  21.7 11.4 %collective-permute-start.4 = (bf16[1,2,2,128,128]{4,3,2,1,0:T(8,128)(2,1)S(1)}, bf16[1,2,2,128,128]{4,3,2,1,0:T(8,128)(2,1)S(1)}, u32[]{:S(2)}, u32[]{:S(2)}) collective-permute-start(bf16[1,2,2,128,128]{4,3,2,1,0:T(8,128)(2,1)S(1)} %maximum_bitcast_fusion), channel_id=1, source_target_pairs={{0,4},{1,5},{2,6},{3,7},{4,0},{5,1},{6,2},{7,3},{8,12},{9,13},{10,... | collective-permute-start | bytes 393224 | tf_op jit(solution)/shard_map/keys_z1/ppermute | solution.py:43
  33.2 10.2 %collective-permute-start.5 = (bf16[2,2,2,128,128]{4,3,2,1,0:T(8,128)(2,1)S(1)}, bf16[2,2,2,128,128]{4,3,2,1,0:T(8,128)(2,1)S(1)}, u32[]{:S(2)}, u32[]{:S(2)}) collective-permute-start(bf16[2,2,2,128,128]{4,3,2,1,0:T(8,128)(2,1)S(1)} %pad_maximum_fusion.4), channel_id=1, source_target_pairs={{0,2},{1,3},{2,0},{3,1},{4,6},{5,7},{6,4},{7,5},{8,10},{9,11},{10,... | collective-permute-start | bytes 786440 | tf_op jit(solution)/shard_map/keys_z2/ppermute | solution.py:43
  43.5 18.2 %copy-start.2 = (bf16[4,2,2,128,128]{4,3,2,1,0:T(8,128)(2,1)}, bf16[4,2,2,128,128]{4,3,2,1,0:T(8,128)(2,1)S(1)}, u32[]{:S(2)}) copy-start(bf16[4,2,2,128,128]{4,3,2,1,0:T(8,128)(2,1)S(1)} %pad_maximum_fusion.3.refs_0_) | copy-start | bytes 1572868
  43.5 12.7 %collective-permute-start.6 = (bf16[4,2,2,128,128]{4,3,2,1,0:T(8,128)(2,1)S(1)}, bf16[4,2,2,128,128]{4,3,2,1,0:T(8,128)(2,1)}, u32[]{:S(2)}, u32[]{:S(2)}) collective-permute-start(bf16[4,2,2,128,128]{4,3,2,1,0:T(8,128)(2,1)S(1)} %pad_maximum_fusion.3.refs_0_), channel_id=1, source_target_pairs={{0,8},{1,9},{2,10},{3,11},{4,12},{5,13},{6,14},{7,15},{8,0},{9,1},... | collective-permute-start | bytes 1572872 | tf_op jit(solution)/shard_map/keys_y1/ppermute | solution.py:43
  47.6 20.1 %collective-permute-start.1 = (bf16[2,144,1024]{2,1,0:T(8,128)(2,1)S(1)}, bf16[2,144,1024]{2,1,0:T(8,128)(2,1)}, u32[]{:S(2)}, u32[]{:S(2)}) collective-permute-start(bf16[2,144,1024]{2,1,0:T(8,128)(2,1)S(1)} %pad_maximum_fusion.2), channel_id=1, source_target_pairs={{0,64},{1,65},{2,66},{3,67},{4,68},{5,69},{6,70},{7,71},{8,72},{9,... | collective-permute-start | bytes 1769480 | tf_op jit(solution)/shard_map/queries_2/ppermute | solution.py:43
  58.4 30.2 %collective-permute-start.7 = (bf16[8,2,2,128,128]{4,3,2,1,0:T(8,128)(2,1)}, bf16[8,2,2,128,128]{4,3,2,1,0:T(8,128)(2,1)}, u32[]{:S(2)}, u32[]{:S(2)}) collective-permute-start(bf16[8,2,2,128,128]{4,3,2,1,0:T(8,128)(2,1)} %pad_maximum_fusion.1), channel_id=1, source_target_pairs={{0,24},{1,25},{2,26},{3,27},{4,28},{5,29},{6,30},{7,31},{8,16},{9,... | collective-permute-start | bytes 3145736 | tf_op jit(solution)/shard_map/keys_y2/ppermute | solution.py:43
  61.7 9.5 %collective-permute-start.8 = (bf16[4,2,2,128,128]{4,3,2,1,0:T(8,128)(2,1)S(1)}, bf16[4,2,2,128,128]{4,3,2,1,0:T(8,128)(2,1)S(1)}, u32[]{:S(2)}, u32[]{:S(2)}) collective-permute-start(bf16[4,2,2,128,128]{4,3,2,1,0:T(8,128)(2,1)S(1)} %pad_maximum_fusion.3.refs_0_), channel_id=1, source_target_pairs={{0,32},{1,33},{2,34},{3,35},{4,36},{5,37},{6,38},{7,39},{8,40},{9,... | collective-permute-start | bytes 1572872 | tf_op jit(solution)/shard_map/keys_c0/ppermute | solution.py:43
  69.0 13.7 %collective-permute-start.9 = (bf16[4,2,2,128,128]{4,3,2,1,0:T(8,128)(2,1)}, bf16[4,2,2,128,128]{4,3,2,1,0:T(8,128)(2,1)}, u32[]{:S(2)}, u32[]{:S(2)}) collective-permute-start(bf16[4,2,2,128,128]{4,3,2,1,0:T(8,128)(2,1)} %collective-permute-done.6.refs_0_), channel_id=1, source_target_pairs={{0,32},{1,33},{2,34},{3,35},{4,36},{5,37},{6,38},{7,39},{8,40},{9,... | collective-permute-start | bytes 1572872 | tf_op jit(solution)/shard_map/keys_c1/ppermute | solution.py:43
  71.2 0.8 copy-start.4
  72.0 1.0 copy-start.3
  73.0 1.0 copy-start.5
  87.3 1.3 %copy-start = (f32[4,128,1024]{2,1,0:T(8,128)}, f32[4,128,1024]{2,1,0:T(8,128)S(1)}, u32[]{:S(2)}) copy-start(f32[4,128,1024]{2,1,0:T(8,128)S(1)} %get-tuple-element.33.refs_8_) | copy-start | bytes 6291460
  88.6 8.4 %collective-permute-start.10 = (bf16[8,2,2,128,128]{4,3,2,1,0:T(8,128)(2,1)}, bf16[8,2,2,128,128]{4,3,2,1,0:T(8,128)(2,1)}, u32[]{:S(2)}, u32[]{:S(2)}) collective-permute-start(bf16[8,2,2,128,128]{4,3,2,1,0:T(8,128)(2,1)} %collective-permute-done.7.refs_0_), channel_id=1, source_target_pairs={{0,32},{1,33},{2,34},{3,35},{4,36},{5,37},{6,38},{7,39},{8,40},{9,... | collective-permute-start | bytes 3145736 | tf_op jit(solution)/shard_map/keys_c2/ppermute | solution.py:43
  91.0 6.0 %copy-start.1 = (f32[4,128,1024]{2,1,0:T(8,128)S(1)}, f32[4,128,1024]{2,1,0:T(8,128)}, u32[]{:S(2)}) copy-start(f32[4,128,1024]{2,1,0:T(8,128)} %copy-done) | copy-start | bytes 6291460
  99.3 18.8 %collective-permute-start.11 = (bf16[144,1024]{1,0:T(8,128)(2,1)S(1)}, bf16[144,1024]{1,0:T(8,128)(2,1)S(1)}, u32[]{:S(2)}, u32[]{:S(2)}) collective-permute-start(bf16[144,1024]{1,0:T(8,128)(2,1)S(1)} %last.4), channel_id=1, source_target_pairs={{0,65},{1,64},{2,67},{3,66},{4,69},{5,68},{6,71},{7,70},{8,73},{9,... | collective-permute-start | bytes 884744 | tf_op jit(solution)/shard_map/sums/ppermute | solution.py:43
  106.6 11.4 %collective-permute-start.12 = (bf16[144,1024]{1,0:T(8,128)(2,1)S(1)}, bf16[144,1024]{1,0:T(8,128)(2,1)S(1)}, u32[]{:S(2)}, u32[]{:S(2)}) collective-permute-start(bf16[144,1024]{1,0:T(8,128)(2,1)S(1)} %last.5), channel_id=1, source_target_pairs={{0,64},{1,65},{2,66},{3,67},{4,68},{5,69},{6,70},{7,71},{8,72},{9,... | collective-permute-start | bytes 884744 | tf_op jit(solution)/shard_map/sums/ppermute | solution.py:43
  112.9 8.6 %collective-permute-start.13 = (bf16[144,1024]{1,0:T(8,128)(2,1)S(1)}, bf16[144,1024]{1,0:T(8,128)(2,1)S(1)}, u32[]{:S(2)}, u32[]{:S(2)}) collective-permute-start(bf16[144,1024]{1,0:T(8,128)(2,1)S(1)} %last.6), channel_id=1, source_target_pairs={{0,1},{1,0},{2,3},{3,2},{4,5},{5,4},{6,7},{7,6},{8,9},{9,8},{10,11... | collective-permute-start | bytes 884744 | tf_op jit(solution)/shard_map/sums/ppermute | solution.py:43
